TPU v7x, 32 devices: a whole 2x2x4 slice. The times are simulated.
32 devices in a mesh: row: 8 (over z, y), col: 4 (over x, core).
Axes of the slice: x: 2, y: 2, z: 4, core: 2. Of those that a mesh axis runs over, the one named last changes fastest.
Arguments:
- features: bfloat16 [8192, 256], P('row', 'col'), may hold values from -600 to 600
- tile_vals: bfloat16 [1280, 128, 128], P('row'), may hold values from -0.125 to 0.125
- tile_rows: int32 [8, 160], P('row'), may hold values from 0 to 7
- tile_srcs: int32 [8, 160], P('row'), may hold values from 0 to 23, as said below
- tile_count: int32 [8], P('row'), may hold values from 20 to 160, as said below
- needed: int32 [8, 8, 2], P('row'), may hold values from 0 to 7, as said below
- hop_noise: float32 [2, 8192, 256], P(None, 'row', 'col'), may hold values from -0.24 to 0.24
- enc_weight: bfloat16 [3, 256, 256], replicated, may hold values from -3.59375 to 3.59375
Outputs:
- encoded: bfloat16 [8192, 256], P('row', 'col')
Inputs may be any that keep to these rules, and one draw needn't show every extreme that they name: `tile_count`: some row index has exactly 160 live slots; slots at or beyond a row index's count are ignored. `tile_srcs`: A value s below 8 names the row index's own block s; otherwise s = 8 + o * 2 + c names entry c of needed for owner o, and o is never the row index itself. needed[d, o, :] are 2 distinct block indices among owner o's 8 blocks.
All inputs are finite; a program needn't handle non-finite values.
Results may differ from a plain program's by a relative error of at most 0.0053.
Values may be sent and summed in bfloat16 or wider, within the bound.
A program may use at most 64 MiB of HBM per device.

v0:
```python
import jax
import jax.numpy as jnp
from jax import lax
from jax.sharding import PartitionSpec as P

BLK = 128
BPD = 8
TPD = 160
CAP = 2
HOPS = 2


epsilon = 1e-06


def shards(features, tile_vals, tile_rows, tile_srcs, tile_count, needed, hop_noise, enc_weight):
    row_count = lax.axis_size("row")
    row_index = lax.axis_index("row")
    col_index = lax.axis_index("col")
    local_rows, local_width = features.shape
    sources = tile_srcs[0]
    block_rows = tile_rows[0]
    live_count = tile_count[0]
    wanted = needed[0]
    tile_order = jnp.arange(TPD, dtype=jnp.int32)
    onehot = (
        (block_rows[:, None] == jnp.arange(BPD, dtype=jnp.int32)[None, :])
        & (tile_order < live_count)[:, None]
    ).astype(jnp.float32)

    def normalize(values):
        squares = lax.psum(jnp.sum(values * values, axis=1), "col")
        return (values / jnp.sqrt(squares + epsilon)[:, None]).astype(jnp.bfloat16)

    remote = jnp.maximum(sources - BPD, 0)
    slot_table = wanted.reshape(-1)
    looked_up = jnp.sum(
        jnp.where(
            remote[:, None] == jnp.arange(row_count * CAP, dtype=jnp.int32)[None, :],
            slot_table[None, :],
            0,
        ),
        axis=1,
    )
    global_block = jnp.where(
        sources < BPD, row_index * BPD + sources, remote // CAP * BPD + looked_up
    )
    current = normalize(features.astype(jnp.float32))
    layers = [current]
    for hop_index in range(HOPS):
        whole = lax.all_gather(current.reshape(BPD, BLK * local_width), "row", axis=0, tiled=True)
        products = jnp.einsum(
            "tij,tjf->tif",
            tile_vals,
            jnp.take(whole, global_block, axis=0).reshape(TPD, BLK, local_width),
            preferred_element_type=jnp.float32,
        )
        summed = jnp.einsum("tr,tif->rif", onehot, products, precision=lax.Precision.HIGHEST)
        current = normalize(summed.reshape(local_rows, local_width) + hop_noise[hop_index])
        layers.append(current)
    stacked = jnp.stack(layers)
    weight_slice = lax.dynamic_slice_in_dim(
        enc_weight, col_index * local_width, local_width, axis=1
    )
    terms = jnp.einsum("kri,kio->ro", stacked, weight_slice, preferred_element_type=jnp.float32)
    encoded = lax.psum_scatter(terms, "col", scatter_dimension=1, tiled=True)
    return encoded.astype(jnp.bfloat16)


def solution(mesh):
    in_specs = (
        P("row", "col"),
        P("row", None, None),
        P("row", None),
        P("row", None),
        P("row"),
        P("row", None, None),
        P(None, "row", "col"),
        P(),
    )
    out_specs = P("row", "col")
    return jax.shard_map(shards, mesh=mesh, in_specs=in_specs, out_specs=out_specs, check_vma=False)
```

profile of v0, /device:TPU:1, one launch (start us, length us, event | category | flops | bytes accessed | tf_op | source)
XLA Modules:
  0.0 202.6 jit_solution(10975890000151822481)
XLA Ops:
  6.5 1.0 fusion.9
  7.5 6.4 %psum.21 = f32[1024]{0:T(1024)S(1)} all-reduce(f32[1024]{0:T(1024)S(1)} %fusion.9), channel_id=1, replica_groups=mesh['row'=8,'col'=4] {'col'}, use_global_device_ids=true, to_apply=%region_1.2 | all-reduce | flops 1024 | bytes 8192 | tf_op jit(solution)/shard_map/psum | solution.py:32
  13.9 0.9 fusion.10
  15.1 0.9 reshape.66
  16.1 0.8 copy.14
  17.6 1.0 slice_bitcast_fusion.1
  18.5 0.7 copy.24
  19.3 0.5 iota_compare_fusion.2
  19.8 0.7 compare_reduce_fusion
  20.5 0.7 add_maximum_fusion
  21.3 35.8 %all-gather.3.cloned.1.call-done = bf16[64,8192]{1,0:T(8,128)(2,1)} async-done(((bf16[8,8192]{1,0:T(8,128)(2,1)}), bf16[64,8192]{1,0:T(8,128)(2,1)}) %all-gather.3.cloned.1.call-update) | async-done | bytes 1048592 | tf_op jit(solution)/shard_map/all_gather | solution.py:51
  57.1 5.9 %gather_fusion = bf16[160,8192]{1,0:T(8,128)(2,1)S(1)} fusion(bf16[64,8192]{1,0:T(8,128)(2,1)} %all-gather.3.cloned.1.call-done, s32[1024]{0:T(1024)S(1)} %pad_clamp_fusion), kind=kCustom, calls=%fused_computation.clone | custom fusion | bytes 5243520 | tf_op jit(solution)/shard_map/jit(_take)/gather | solution.py:55
  63.0 1.8 broadcast_select_fusion.1
  64.8 8.4 %reshape.67 = bf16[160,128,64]{2,1,0:T(8,128)(2,1)} reshape(bf16[160,8192]{1,0:T(8,128)(2,1)} %broadcast_select_fusion.1) | data formatting | bytes 5242880 | tf_op jit(solution)/shard_map/reshape | solution.py:55
  73.2 7.7 %convolution_bitcast_fusion.1 = f32[160,128,64]{1,2,0:T(8,128)S(1)} fusion(bf16[160,128,64]{2,1,0:T(8,128)(2,1)} %reshape.67, bf16[160,128,128]{2,1,0:T(8,128)(2,1)} %param.11), kind=kOutput, calls=%fused_computation.9 | convolution fusion | flops 335544320 | bytes 13107200 | tf_op jit(solution)/shard_map/tij,tjf->tif/dot_general | solution.py:52
  81.0 4.7 %fusion.14 = (f32[8,128]{1,0:T(8,128)S(1)}, f32[8,128,64]{1,0,2:T(8,128)S(1)}) fusion(f32[8,8,8,128]{3,2,1,0:T(8,128)S(1)} %copy-done.3, f32[160,128,64]{1,2,0:T(8,128)S(1)} %convolution_bitcast_fusion.1, s32[160]{0:T(256)S(1)} %bitcast.59, pred[160]{0:T(512)(128)(4,1)S(1)} %copy-done.8), kind=kOutput, calls=%fused_computation.25 | convolution fusion | flops 126027264 | bytes 5772064 | tf_op jit(solution)/shard_map/tr,tif->rif/dot_general | solution.py:58
  86.0 6.7 %psum.22 = f32[1024]{0:T(1024)S(1)} all-reduce(f32[1024]{0:T(1024)S(1)} %bitcast.55), channel_id=1, replica_groups=mesh['row'=8,'col'=4] {'col'}, use_global_device_ids=true, to_apply=%region_4.6 | all-reduce | flops 1024 | bytes 8192 | tf_op jit(solution)/shard_map/psum | solution.py:32
  92.7 0.7 divide_convert_fusion.2
  94.4 0.7 divide_convert_fusion.1
  95.1 0.3 reduce-scatter.2.cloned.1.call-start
  95.4 0.7 fusion.31
  96.1 0.7 copy.25
  96.8 36.7 %all-gather.5.cloned.1.call-done = bf16[64,8192]{1,0:T(8,128)(2,1)} async-done(((bf16[8,8192]{1,0:T(8,128)(2,1)}), bf16[64,8192]{1,0:T(8,128)(2,1)}) %all-gather.5.cloned.1.call-update) | async-done | bytes 1048592 | tf_op jit(solution)/shard_map/all_gather | solution.py:51
  133.5 5.9 %gather_fusion.1 = bf16[160,8192]{1,0:T(8,128)(2,1)S(1)} fusion(bf16[64,8192]{1,0:T(8,128)(2,1)} %all-gather.5.cloned.1.call-done, s32[1024]{0:T(1024)S(1)} %pad_clamp_fusion), kind=kCustom, calls=%fused_computation.1.clone | custom fusion | bytes 5243520 | tf_op jit(solution)/shard_map/jit(_take)/gather | solution.py:55
  139.4 1.8 broadcast_select_fusion
  141.3 8.4 %reshape.70 = bf16[160,128,64]{2,1,0:T(8,128)(2,1)} reshape(bf16[160,8192]{1,0:T(8,128)(2,1)} %broadcast_select_fusion) | data formatting | bytes 5242880 | tf_op jit(solution)/shard_map/reshape | solution.py:55
  149.7 7.7 %convolution_bitcast_fusion = f32[160,128,64]{1,2,0:T(8,128)S(1)} fusion(bf16[160,128,64]{2,1,0:T(8,128)(2,1)} %reshape.70, bf16[160,128,128]{2,1,0:T(8,128)(2,1)} %param.11), kind=kOutput, calls=%fused_computation.8 | convolution fusion | flops 335544320 | bytes 13107200 | tf_op jit(solution)/shard_map/tij,tjf->tif/dot_general | solution.py:52
  157.4 4.7 %fusion.12 = (f32[8,128]{1,0:T(8,128)S(1)}, f32[8,128,64]{1,0,2:T(8,128)S(1)}) fusion(f32[8,8,8,128]{3,2,1,0:T(8,128)S(1)} %copy-done.4, f32[160,128,64]{1,2,0:T(8,128)S(1)} %convolution_bitcast_fusion, s32[160]{0:T(256)S(1)} %bitcast.60, pred[160]{0:T(512)(128)(4,1)S(1)} %copy-done.9), kind=kOutput, calls=%fused_computation.22 | convolution fusion | flops 126027264 | bytes 5772064 | tf_op jit(solution)/shard_map/tr,tif->rif/dot_general | solution.py:58
  162.2 6.7 %psum.23 = f32[1024]{0:T(1024)S(1)} all-reduce(f32[1024]{0:T(1024)S(1)} %bitcast.56), channel_id=1, replica_groups=mesh['row'=8,'col'=4] {'col'}, use_global_device_ids=true, to_apply=%region_6.8 | all-reduce | flops 1024 | bytes 8192 | tf_op jit(solution)/shard_map/psum | solution.py:32
  169.0 1.3 convolution_bitcast_fusion.2
  170.4 24.0 %reduce-scatter.2.cloned.1.call-done = f32[1024,64]{0,1:T(8,128)} async-done(((f32[1024,256]{0,1:T(8,128)}), f32[1024,64]{0,1:T(8,128)}) %reduce-scatter.2.cloned.1.call-update) | async-done | bytes 262160 | tf_op jit(solution)/shard_map/reduce_scatter | solution.py:66
  194.4 1.6 convert_element_type.26
  (42 shorter events, 1.8 us)
Async XLA Ops:
  6.5 162.4 %copy-start = (bf16[3,256,256]{2,1,0:T(8,128)(2,1)S(1)}, bf16[3,256,256]{2,1,0:T(8,128)(2,1)}, u32[]{:S(2)}) copy-start(bf16[3,256,256]{2,1,0:T(8,128)(2,1)} %param.17) | copy-start | bytes 1179652
  6.5 50.5 %all-gather.3.cloned.1.call-start = ((), (), s32[]{:S(2)}) async-start(), calls=%async_computation.1 | async-start | bytes 1179648 | tf_op jit(solution)/shard_map/all_gather | solution.py:51
  16.0 117.5 %all-gather.5.cloned.1.call-start = ((), (), s32[]{:S(2)}) async-start(), calls=%async_computation.2 | async-start | bytes 1179648 | tf_op jit(solution)/shard_map/all_gather | solution.py:51
  73.2 7.7 %copy-start.3 = (f32[8,8,8,128]{3,2,1,0:T(8,128)S(1)}, f32[8,8,8,128]{3,2,1,0:T(8,128)}, u32[]{:S(2)}) copy-start(f32[8,8,8,128]{3,2,1,0:T(8,128)} %copy.24) | copy-start | bytes 786436
  73.2 7.7 %copy-start.7 = (s32[1,160]{1,0:T(1,128)S(1)}, s32[1,160]{1,0:T(1,128)}, u32[]{:S(2)}) copy-start(s32[1,160]{1,0:T(1,128)} %param.12) | copy-start | bytes 1924
  73.2 7.7 %copy-start.8 = (pred[160]{0:T(512)(128)(4,1)S(1)}, pred[160]{0:T(512)(128)(4,1)}, u32[]{:S(2)}) copy-start(pred[160]{0:T(512)(128)(4,1)} %iota_compare_fusion.2) | copy-start | bytes 484
  80.9 11.8 %copy-start.1 = (f32[2,1024,64]{1,2,0:T(8,128)S(1)}, f32[2,1024,64]{1,2,0:T(8,128)}, u32[]{:S(2)}) copy-start(f32[2,1024,64]{1,2,0:T(8,128)} %param.16) | copy-start | bytes 1572868
  81.0 14.4 %copy-start.2 = (bf16[1024,64]{0,1:T(8,128)(2,1)S(1)}, bf16[1024,64]{0,1:T(8,128)(2,1)}, u32[]{:S(2)}) copy-start(bf16[1024,64]{0,1:T(8,128)(2,1)} %param.10) | copy-start | bytes 393220
  95.1 99.3 %reduce-scatter.2.cloned.1.call-start = ((), (), s32[]{:S(2)}) async-start(), calls=%async_computation.3 | async-start | bytes 1310720 | tf_op jit(solution)/shard_map/reduce_scatter | solution.py:66
  149.7 7.7 %copy-start.4 = (f32[8,8,8,128]{3,2,1,0:T(8,128)S(1)}, f32[8,8,8,128]{3,2,1,0:T(8,128)}, u32[]{:S(2)}) copy-start(f32[8,8,8,128]{3,2,1,0:T(8,128)} %copy.25) | copy-start | bytes 786436
  149.7 7.7 %copy-start.9 = (pred[160]{0:T(512)(128)(4,1)S(1)}, pred[160]{0:T(512)(128)(4,1)}, u32[]{:S(2)}) copy-start(pred[160]{0:T(512)(128)(4,1)} %iota_compare_fusion.2) | copy-start | bytes 484
  157.4 11.6 %copy-start.5 = (bf16[1,1024,64]{1,2,0:T(8,128)(2,1)S(1)}, bf16[1,1024,64]{1,2,0:T(8,128)(2,1)}, u32[]{:S(2)}) copy-start(bf16[1,1024,64]{1,2,0:T(8,128)(2,1)} %fusion.31) | copy-start | bytes 393220
  157.4 11.6 %copy-start.6 = (bf16[1,1024,64]{1,2,0:T(8,128)(2,1)S(1)}, bf16[1,1024,64]{1,2,0:T(8,128)(2,1)}, u32[]{:S(2)}) copy-start(bf16[1,1024,64]{1,2,0:T(8,128)(2,1)} %get-tuple-element.8) | copy-start | bytes 393220
Sparse Core Ops, SparseCore 0:
  16.1 40.8 all-gather.2
  95.2 38.2 all-gather.4
  170.5 23.8 reduce-scatter.1
where the time goes:
time: 204 us; the launch traced here: 203 us
  waiting for transfers between devices  96.5 us (47%)
  local copies, waits for them, and re-layouts  34.4 us (17%)
  matrix products  26.2 us (13%)
  blocking collectives  19.8 us (10%)
  between operations  14 us (7%)
  other arithmetic  11.4 us (6%)
    all_gather x2, waiting for transfers between devices, shards(): lax.all_gather(current.reshape(BPD, BLK * local_width), 'row', axis=0, ti...  72.4 us
    reduce_scatter x1, waiting for transfers between devices, shards(): encoded = lax.psum_scatter(terms, 'col', scatter_dimension=1, tiled=True)  24 us
    psum x3, blocking collectives, normalize(): squares = lax.psum(jnp.sum(values * values, axis=1), 'col')  19.8 us
    reshape x2, local copies, waits for them, and re-layouts, shards(): jnp.take(whole, global_block, axis=0).reshape(TPD, BLK, local_width)  16.8 us
    dot_general x2, matrix products, shards(): jnp.einsum('tij,tjf->tif', tile_vals, jnp.take(whole, global_block, axis=...  15.4 us
    gather x2, local copies, waits for them, and re-layouts, shards(): jnp.take(whole, global_block, axis=0).reshape(TPD, BLK, local_width)  11.9 us
    dot_general x2, matrix products, shards(): jnp.einsum('tr,tif->rif', onehot, products, precision=lax.Precision.HIGHEST)  9.47 us
  transfers between devices with their start and end apart: 3, of which 3 were waited for; matrix products, arithmetic and copies ran while one was open for 3% of the time, Pallas kernels for 0%

commit v1 on v0

v1 whole, which is shorter than its diff:
```python
import functools

import jax
import jax.numpy as jnp
from jax import lax
from jax.experimental import pallas as pl
from jax.experimental.pallas import tpu as pltpu
from jax.sharding import PartitionSpec as P

BLK = 128
BPD = 8
CAP = 2
HOPS = 2
PAIRS = BPD // 2
MESH = pl.DeviceIdType.MESH
EPSILON = 1e-06


def kernel(n, nc, prev, head, wanted, feat, tiles, noise, weight, out,
           vals, sums, dense, noise_v, weight_v, squares, xs, hd, send, recv, wanted_v, wanted_s,
           heads, head_w, acc, enc,
           local_sem, wanted_send, wanted_recv, sq_send, sq_recv, row_send, row_recv, col_send, col_recv, table_sem):
    me = lax.axis_index("row")
    col = lax.axis_index("col")
    width = feat.shape[1]
    slots = vals.shape[0]
    f32, bf16 = jnp.float32, jnp.bfloat16

    vals_copy = pltpu.make_async_copy(tiles, vals, local_sem.at[0])
    noise_copy = pltpu.make_async_copy(noise, noise_v, local_sem.at[1])
    weight_copy = pltpu.make_async_copy(weight, weight_v, local_sem.at[2])
    vals_copy.start()
    noise_copy.start()
    weight_copy.start()

    barrier = pltpu.get_barrier_semaphore()

    def greet_row(k, c):
        pl.semaphore_signal(barrier, inc=1, device_id={"row": lax.rem(me + k, n)}, device_id_type=MESH)
        return c

    lax.fori_loop(1, n, greet_row, 0)
    for k in range(1, nc):
        pl.semaphore_signal(barrier, inc=1, device_id={"col": lax.rem(col + k, nc)}, device_id_type=MESH)

    left = lax.broadcasted_iota(jnp.int32, (BLK, 2 * width), 1) < width
    zero_tile = jnp.zeros((BLK, 2 * width), f32)

    def stat(stage, x):
        for j in range(PAIRS):
            t = (x[j] * x[j]).T
            squares[stage, 0, 2 * j : 2 * j + 1, :] = jnp.sum(t[:width], axis=0, keepdims=True)
            squares[stage, 0, 2 * j + 1 : 2 * j + 2, :] = jnp.sum(t[width:], axis=0, keepdims=True)
            xs[j] = x[j]

    def square_copy(stage, k):
        return pltpu.make_async_remote_copy(
            src_ref=squares.at[stage, 0], dst_ref=squares.at[stage, k],
            send_sem=sq_send.at[stage, k], recv_sem=sq_recv.at[stage, k],
            device_id={"col": lax.rem(col + k, nc)}, device_id_type=MESH)

    def head_copy(stage, k):
        return pltpu.make_async_remote_copy(
            src_ref=heads.at[stage, 0], dst_ref=heads.at[stage, k],
            send_sem=col_send.at[stage, k], recv_sem=col_recv.at[stage, k],
            device_id={"col": lax.rem(col + k, nc)}, device_id_type=MESH)

    def wanted_copy(k):
        peer = lax.rem(me + k, n)
        return pltpu.make_async_remote_copy(
            src_ref=wanted.at[peer], dst_ref=wanted_v.at[k],
            send_sem=wanted_send.at[k], recv_sem=wanted_recv.at[k],
            device_id={"row": peer}, device_id_type=MESH)

    def row_copy(hop, k):
        return pltpu.make_async_remote_copy(
            src_ref=send.at[k], dst_ref=recv.at[hop, k],
            send_sem=row_send.at[hop, k], recv_sem=row_recv.at[hop, k],
            device_id={"row": lax.rem(me + k, n)}, device_id_type=MESH)

    def row_loop(body):
        def step(k, c):
            body(k)
            return c
        lax.fori_loop(1, n, step, 0)

    def normalized(stage):
        for k in range(1, nc):
            square_copy(stage, k).wait_recv()
        total = squares[stage, 0]
        for k in range(1, nc):
            total = total + squares[stage, k]
        inverse = 1.0 / jnp.sqrt(total + EPSILON)
        for j in range(PAIRS):
            both = jnp.concatenate(
                [jnp.broadcast_to(inverse[2 * j : 2 * j + 1], (width, BLK)),
                 jnp.broadcast_to(inverse[2 * j + 1 : 2 * j + 2], (width, BLK))], axis=0).T
            h = (xs[j] * both).astype(bf16)
            heads[stage, 0, j] = h
            if stage < HOPS:
                h = h.astype(f32)
                turned = pltpu.roll(h, width, 1)
                hd[2 * j] = jnp.where(left, h, turned).astype(bf16)
                hd[2 * j + 1] = jnp.where(left, turned, h).astype(bf16)

    def send_rows(hop):
        def body(k):
            first = wanted_s[n - k, 0, 0]
            second = wanted_s[n - k, 0, 1]
            a = hd[first].astype(f32)
            b = hd[second].astype(f32)
            if hop > 0:
                row_copy(hop - 1, k).wait_send()
            send[k] = jnp.where(left, a, b).astype(bf16)
            row_copy(hop, k).start()
        row_loop(body)

    def spread(packed):
        p = packed.astype(f32)
        return jnp.concatenate([jnp.where(left, p, 0.0), jnp.where(left, 0.0, p)], axis=0).astype(bf16)

    def add_encoded(stage, k):
        source = lax.rem(col + nc - k, nc)
        e = head_w[stage, pl.ds(pl.multiple_of(source * width, width), width), :].astype(f32)
        mask = left[:width]
        w = jnp.concatenate([jnp.where(mask, e, 0.0), jnp.where(mask, 0.0, e)], axis=0).astype(bf16)
        enc[...] += jnp.dot(heads[stage, k].reshape(PAIRS * BLK, 2 * width), w, preferred_element_type=f32)

    diag = lax.broadcasted_iota(jnp.int32, (width, 2 * width), 0)
    lane = lax.broadcasted_iota(jnp.int32, (width, 2 * width), 1)
    twice = ((lane == diag) | (lane == diag + width)).astype(f32).astype(bf16)
    x = []
    for j in range(PAIRS):
        both = jnp.dot(feat[2 * j * BLK : (2 * j + 2) * BLK, :], twice, preferred_element_type=f32)
        x.append(jnp.where(left, both[:BLK], both[BLK:]))
    stat(0, x)

    pl.semaphore_wait(barrier, n - 1 + nc - 1)
    for k in range(1, nc):
        square_copy(0, k).start()
    row_loop(lambda k: wanted_copy(k).start())
    sums[slots] = zero_tile
    row_loop(lambda k: wanted_copy(k).wait_recv())
    table = pltpu.make_async_copy(wanted_v.at[pl.ds(1, n - 1)], wanted_s.at[pl.ds(1, n - 1)], table_sem.at[0])
    table.start()
    normalized(0)
    table.wait()
    send_rows(0)
    for k in range(1, nc):
        head_copy(0, k).start()

    vals_copy.wait()

    def link(t, c):
        sums[t] = vals[t].astype(f32) + sums[prev[t]]
        return c

    lax.fori_loop(0, slots, link, 0, unroll=4)

    def lay(q, c):
        for r in range(BPD):
            for h in range(2):
                dense[q, r * BLK : (r + 1) * BLK, h * BLK : (h + 1) * BLK] = (
                    sums[head[(2 * q + h) * BPD + r]].astype(bf16))
        return c

    lax.fori_loop(0, dense.shape[0], lay, 0)

    weight_copy.wait()
    depth = weight_v.shape[1]
    pick_row = lax.broadcasted_iota(jnp.int32, (depth, 2 * width), 0) - col * width
    pick_lane = lax.broadcasted_iota(jnp.int32, (depth, 2 * width), 1)
    pick = ((pick_lane == pick_row) | (pick_lane == pick_row + width)).astype(f32)
    pick = jnp.where((pick_row >= 0) & (pick_row < width), pick, 0.0).astype(bf16)
    for stage in range(HOPS + 1):
        head_w[stage] = jnp.dot(weight_v[stage], pick, preferred_element_type=f32).astype(bf16)
    enc[...] = jnp.zeros_like(enc)
    noise_copy.wait()

    for hop in range(HOPS):
        acc[...] = jnp.dot(dense[0], spread(heads[hop, 0, 0]), preferred_element_type=f32)
        for j in range(1, PAIRS):
            acc[...] += jnp.dot(dense[j], spread(heads[hop, 0, j]), preferred_element_type=f32)
        add_encoded(hop, 0)
        if hop > 0:
            for k in range(1, nc):
                head_copy(hop - 1, k).wait_recv()
                add_encoded(hop - 1, k)

        def arrive(k):
            row_copy(hop, k).wait_recv()
            owner = lax.rem(me + n - k, n)
            acc[...] += jnp.dot(dense[PAIRS + owner], spread(recv[hop, k]), preferred_element_type=f32)

        row_loop(arrive)
        x = []
        for j in range(PAIRS):
            a = acc[2 * j * BLK : (2 * j + 1) * BLK, :]
            b = acc[(2 * j + 1) * BLK : (2 * j + 2) * BLK, :]
            g = jnp.where(left, a, b) + pltpu.roll(jnp.where(left, b, a), width, 1)
            z = jnp.concatenate(
                [noise_v[hop, 2 * j * BLK : (2 * j + 1) * BLK, :],
                 noise_v[hop, (2 * j + 1) * BLK : (2 * j + 2) * BLK, :]], axis=1)
            x.append(g + z)
        stat(hop + 1, x)
        for k in range(1, nc):
            square_copy(hop + 1, k).start()
        normalized(hop + 1)
        if hop + 1 < HOPS:
            send_rows(hop + 1)
        for k in range(1, nc):
            head_copy(hop + 1, k).start()

    add_encoded(HOPS, 0)
    for stage in (HOPS - 1, HOPS):
        for k in range(1, nc):
            head_copy(stage, k).wait_recv()
            add_encoded(stage, k)
    for j in range(PAIRS):
        e = enc[j * BLK : (j + 1) * BLK, :]
        out[2 * j * BLK : (2 * j + 1) * BLK, :] = e[:, :width].astype(bf16)
        out[(2 * j + 1) * BLK : (2 * j + 2) * BLK, :] = pltpu.roll(e, width, 1)[:, :width].astype(bf16)

    row_loop(lambda k: wanted_copy(k).wait_send())
    row_loop(lambda k: row_copy(HOPS - 1, k).wait_send())
    for stage in range(HOPS + 1):
        for k in range(1, nc):
            square_copy(stage, k).wait_send()
            head_copy(stage, k).wait_send()


def shards(n, nc, features, tile_vals, tile_rows, tile_srcs, tile_count, needed, hop_noise, enc_weight):
    local_rows, width = features.shape
    slots = tile_vals.shape[0]
    cells = (BPD + n * CAP) * BPD
    order = jnp.arange(slots, dtype=jnp.int32)
    cell = tile_srcs[0] * BPD + tile_rows[0]
    same = (cell[:, None] == cell[None, :]) & (order[None, :] < order[:, None])
    prev = jnp.max(jnp.where(same, order[None, :], -1), axis=1)
    prev = jnp.where(prev < 0, slots, prev)
    mine = (cell[None, :] == jnp.arange(cells, dtype=jnp.int32)[:, None]) & (order < tile_count[0])[None, :]
    head = jnp.max(jnp.where(mine, order[None, :], -1), axis=1)
    head = jnp.where(head < 0, slots, head)
    wanted = jnp.pad(needed[0][:, None, :], ((0, 0), (0, 0), (0, BLK - CAP)))
    f32, bf16 = jnp.float32, jnp.bfloat16
    vmem = pl.BlockSpec(memory_space=pltpu.VMEM)
    smem = pl.BlockSpec(memory_space=pltpu.SMEM)
    anyspace = pl.BlockSpec(memory_space=pl.ANY)
    sem = pltpu.SemaphoreType.DMA
    pair = (BLK, 2 * width)
    return pl.pallas_call(
        functools.partial(kernel, n, nc),
        out_shape=jax.ShapeDtypeStruct((local_rows, width), bf16),
        in_specs=[smem, smem, anyspace, vmem, anyspace, anyspace, anyspace],
        out_specs=vmem,
        scratch_shapes=[
            pltpu.VMEM(tile_vals.shape, bf16),
            pltpu.VMEM((slots + 1, BLK, BLK), f32),
            pltpu.VMEM((PAIRS + n, local_rows, 2 * BLK), bf16),
            pltpu.VMEM(hop_noise.shape, f32),
            pltpu.VMEM(enc_weight.shape, bf16),
            pltpu.VMEM((HOPS + 1, nc, BPD, BLK), f32),
            pltpu.VMEM((PAIRS,) + pair, f32),
            pltpu.VMEM((BPD,) + pair, bf16),
            pltpu.VMEM((n,) + pair, bf16),
            pltpu.VMEM((HOPS, n) + pair, bf16),
            pltpu.VMEM((n, 1, BLK), jnp.int32),
            pltpu.SMEM((n, 1, BLK), jnp.int32),
            pltpu.VMEM((HOPS + 1, nc, PAIRS) + pair, bf16),
            pltpu.VMEM((HOPS + 1, enc_weight.shape[1], 2 * width), bf16),
            pltpu.VMEM((local_rows, 2 * width), f32),
            pltpu.VMEM((PAIRS * BLK, 2 * width), f32),
            sem((3,)),
            sem((n,)), sem((n,)),
            sem((HOPS + 1, nc)), sem((HOPS + 1, nc)),
            sem((HOPS, n)), sem((HOPS, n)),
            sem((HOPS + 1, nc)), sem((HOPS + 1, nc)),
            sem((1,)),
        ],
        compiler_params=pltpu.CompilerParams(
            collective_id=0, has_side_effects=True, vmem_limit_bytes=62 * 2**20),
    )(prev, head, wanted, features, tile_vals, hop_noise, enc_weight)


def solution(mesh):
    n, nc = mesh.shape["row"], mesh.shape["col"]
    in_specs = (
        P("row", "col"),
        P("row", None, None),
        P("row", None),
        P("row", None),
        P("row"),
        P("row", None, None),
        P(None, "row", "col"),
        P(),
    )
    return jax.shard_map(functools.partial(shards, n, nc), mesh=mesh, in_specs=in_specs,
                         out_specs=P("row", "col"), check_vma=False)
```

time: 204 us -> 52 us (0.25)
  waiting for transfers between devices: 96.5 us -> 0 us
  Pallas kernels: 0 us -> 41.7 us
  local copies, waits for them, and re-layouts: 34.4 us -> 7.21 us
  matrix products: 26.2 us -> 0 us
  blocking collectives: 19.8 us -> 0 us
  between operations: 14 us -> 0.68 us
  other arithmetic: 11.4 us -> 2.18 us
    all_gather x2 -> x0, waiting for transfers between devices: 72.4 us -> none  [shards(): lax.all_gather(current.reshape(BPD, BLK * local_width), 'row', axis=0, ti...]
    pallas_call x0 -> x1, Pallas kernels: none -> 41.7 us  [shards(): pl.pallas_call(functools.partial(kernel, n, nc), out_shape=jax.ShapeDtype...]
    dot_general x5 -> x0, matrix products: 26.2 us -> none  [the longest x2 15.4 us: shards(): jnp.einsum('tij,tjf->tif', tile_vals, jnp.take(whole, global_block, axis=...]
    reduce_scatter x1 -> x0, waiting for transfers between devices: 24 us -> none  [shards(): encoded = lax.psum_scatter(terms, 'col', scatter_dimension=1, tiled=True)]
    psum x3 -> x0, blocking collectives: 19.8 us -> none  [normalize(): squares = lax.psum(jnp.sum(values * values, axis=1), 'col')]
    reshape x6 -> x0, local copies, waits for them, and re-layouts: 18 us -> none  [the longest x2 16.8 us: shards(): jnp.take(whole, global_block, axis=0).reshape(TPD, BLK, local_width)]
    gather x2 -> x0, local copies, waits for them, and re-layouts: 11.9 us -> none  [shards(): jnp.take(whole, global_block, axis=0).reshape(TPD, BLK, local_width)]
    convert_element_type x5 -> x0, other arithmetic: 4.03 us -> none  [the longest x4 2.41 us: normalize(): return (values / jnp.sqrt(squares + epsilon)[:, None]).astype(jnp.bfloat16)]
  transfers between devices with their start and end apart: 3 -> 0, of which waited for: 3 -> 0; matrix products, arithmetic and copies ran while one was open for 3% -> 0% of each run, Pallas kernels for 0% -> 0%
where the time goes in v1:
time: 52 us; the launch traced here: 51.7 us
  Pallas kernels  41.7 us (80%)
  local copies, waits for them, and re-layouts  7.21 us (14%)
  other arithmetic  2.18 us (4%)
  between operations  0.68 us (1%)
    pallas_call x1, Pallas kernels, shards(): pl.pallas_call(functools.partial(kernel, n, nc), out_shape=jax.ShapeDtype...  41.7 us
    unnamed x2, local copies, waits for them, and re-layouts  4.13 us
    pallas_call x1, local copies, waits for them, and re-layouts, shards(): pl.pallas_call(functools.partial(kernel, n, nc), out_shape=jax.ShapeDtype...  1.73 us

profile of v1, /device:TPU:1, one launch (start us, length us, event | category | flops | bytes accessed | tf_op | source)
XLA Modules:
  0.0 51.7 jit_solution(16966973872418466640)
XLA Ops:
  0.7 0.7 %multiply_add_fusion = s32[1,160]{1,0:T(1,128)S(1)} fusion(s32[1,160]{1,0:T(1,128)} %param.10, s32[1,160]{1,0:T(1,128)} %param.11), kind=kLoop, calls=%fused_computation.9 | loop fusion | flops 320 | bytes 1920 | tf_op jit(solution)/shard_map/add | solution.py:237
  1.4 0.1 select_reduce_fusion
  1.5 0.2 select_reduce_fusion.1
  1.7 0.6 %compare_select_fusion.1.prev = s32[160]{0:T(256)} fusion(s32[160]{0:T(256)S(1)} %select_reduce_fusion.1), kind=kLoop, calls=%fused_computation.7 | loop fusion | flops 320 | bytes 1280 | tf_op jit(solution)/shard_map/jit(_where)/select_n | solution.py:240
  2.3 0.6 %compare_select_fusion.head = s32[192]{0:T(256)} fusion(s32[192]{0:T(256)S(1)} %select_reduce_fusion), kind=kLoop, calls=%fused_computation.6 | loop fusion | flops 384 | bytes 1536 | tf_op jit(solution)/shard_map/jit(_where)/select_n | solution.py:243
  2.8 0.8 %copy.13 = s32[8,1,2]{2,1,0:T(1,128)S(1)} copy(s32[8,1,2]{0,2,1:T(2,128)} %bitcast.6) | data formatting | bytes 128 | tf_op jit(solution)/shard_map/broadcast_in_dim;squeeze | solution.py:244
  3.6 0.6 %pad.4.wanted = s32[8,1,128]{2,1,0:T(1,128)} pad(s32[8,1,2]{2,1,0:T(1,128)S(1)} %copy.13, s32[]{:T(128)} %constant.1.clone.1), padding=0_0x0_0x0_126 | pad | bytes 4164 | tf_op jit(solution)/shard_map/jit(_pad)/pad | solution.py:244
  4.2 1.8 %copy.14.feat = bf16[1024,64]{1,0:T(8,128)(2,1)} copy(bf16[1024,64]{0,1:T(8,128)(2,1)} %param.8) | data formatting | bytes 262144 | tf_op args[0]
  6.0 2.4 %copy.15.noise = f32[2,1024,64]{2,1,0:T(8,128)} copy(f32[2,1024,64]{1,2,0:T(8,128)} %param.14) | data formatting | bytes 1048576 | tf_op args[6]
  8.3 41.7 %shard_map.82 = bf16[1024,64]{1,0:T(8,128)(2,1)} custom-call(s32[160]{0:T(256)} %compare_select_fusion.1.prev, s32[192]{0:T(256)} %compare_select_fusion.head, s32[8,1,128]{2,1,0:T(1,128)} %pad.4.wanted, bf16[1024,64]{1,0:T(8,128)(2,1)} %copy.14.feat, bf16[160,128,128]{2,1,0:T(8,128)(2,1)} %tiles.1, f32[2,1024,64]{2,1,0:T(8,128)} %copy.15.noise, ...), custom_call_target="tpu_custom_call" | custom-call | tf_op jit(solution)/shard_map/pallas_call | solution.py:251
  50.0 1.7 %copy.16 = bf16[1024,64]{0,1:T(8,128)(2,1)} copy(bf16[1024,64]{1,0:T(8,128)(2,1)} %shard_map.82) | data formatting | bytes 262144 | tf_op jit(solution)/shard_map/pallas_call | solution.py:251
  (1 shorter events, 0.0 us)

commit v2 on v1

v2 whole, which is shorter than its diff:
```python
import functools

import jax
import jax.numpy as jnp
from jax import lax
from jax.experimental import pallas as pl
from jax.experimental.pallas import tpu as pltpu
from jax.sharding import PartitionSpec as P

BLK = 128
BPD = 8
CAP = 2
HOPS = 2
PAIRS = BPD // 2
MESH = pl.DeviceIdType.MESH
EPSILON = 1e-06


def kernel(n, nc, rows, srcs, count, wanted, feat, tiles, noise, weight, out,
           vals, sums, dense, noise_v, weight_v, squares, xs, hp, hd, send, recv, wanted_v, wanted_s,
           cells, links_v, links, heads, head_w, acc, enc,
           local_sem, wanted_send, wanted_recv, sq_send, sq_recv, row_send, row_recv, col_send, col_recv, table_sem):
    me = lax.axis_index("row")
    col = lax.axis_index("col")
    width, nodes = feat.shape
    slots = vals.shape[0]
    f32, bf16 = jnp.float32, jnp.bfloat16

    vals_copy = pltpu.make_async_copy(tiles, vals, local_sem.at[0])
    noise_copy = pltpu.make_async_copy(noise, noise_v, local_sem.at[1])
    weight_copy = pltpu.make_async_copy(weight, weight_v, local_sem.at[2])

    barrier = pltpu.get_barrier_semaphore()

    def row_loop(body):
        def step(k, c):
            body(k)
            return c
        lax.fori_loop(1, n, step, 0)

    row_loop(lambda k: pl.semaphore_signal(
        barrier, inc=1, device_id={"row": lax.rem(me + k, n)}, device_id_type=MESH))
    for k in range(1, nc):
        pl.semaphore_signal(barrier, inc=1, device_id={"col": lax.rem(col + k, nc)}, device_id_type=MESH)
    vals_copy.start()
    noise_copy.start()
    weight_copy.start()

    left = lax.broadcasted_iota(jnp.int32, (BLK, 2 * width), 1) < width

    def block(b):
        return slice(b * BLK, (b + 1) * BLK)

    def stat(stage, x):
        squares[stage, 0] = jnp.sum(x * x, axis=0, keepdims=True)

    def square_copy(stage, k):
        return pltpu.make_async_remote_copy(
            src_ref=squares.at[stage, 0], dst_ref=squares.at[stage, k],
            send_sem=sq_send.at[stage, k], recv_sem=sq_recv.at[stage, k],
            device_id={"col": lax.rem(col + k, nc)}, device_id_type=MESH)

    def head_copy(stage, k, source):
        return pltpu.make_async_remote_copy(
            src_ref=heads.at[stage, source], dst_ref=heads.at[stage, source],
            send_sem=col_send.at[stage, k], recv_sem=col_recv.at[stage, k],
            device_id={"col": lax.rem(col + k, nc)}, device_id_type=MESH)

    def start_heads(stage):
        for k in range(1, nc):
            head_copy(stage, k, col).start()

    def wait_heads(stage):
        for k in range(1, nc):
            head_copy(stage, k, lax.rem(col + nc - k, nc)).wait_recv()

    def wanted_copy(k):
        return pltpu.make_async_remote_copy(
            src_ref=wanted.at[0], dst_ref=wanted_v.at[k],
            send_sem=wanted_send.at[k], recv_sem=wanted_recv.at[k],
            device_id={"row": lax.rem(me + k, n)}, device_id_type=MESH)

    def row_copy(hop, k):
        return pltpu.make_async_remote_copy(
            src_ref=send.at[k], dst_ref=recv.at[hop, k],
            send_sem=row_send.at[hop, k], recv_sem=row_recv.at[hop, k],
            device_id={"row": lax.rem(me + k, n)}, device_id_type=MESH)

    def inverse_norm(stage):
        for k in range(1, nc):
            square_copy(stage, k).wait_recv()
        total = squares[stage, 0]
        for k in range(1, nc):
            total = total + squares[stage, k]
        return 1.0 / jnp.sqrt(total + EPSILON)

    def normalized(stage):
        inverse = inverse_norm(stage)
        for j in range(PAIRS):
            a, b = block(2 * j), block(2 * j + 1)
            ha = (xs[:, a] * inverse[:, a]).astype(bf16)
            hb = (xs[:, b] * inverse[:, b]).astype(bf16)
            heads[stage, col, :, a] = ha
            heads[stage, col, :, b] = hb
            h = jnp.concatenate([ha.astype(f32), hb.astype(f32)], axis=0).T
            hp[j] = h.astype(bf16)
            turned = pltpu.roll(h, width, 1)
            hd[2 * j] = jnp.where(left, h, turned).astype(bf16)
            hd[2 * j + 1] = jnp.where(left, turned, h).astype(bf16)

    def send_rows(hop):
        def body(k):
            first = wanted_s[n - k, 0, me]
            second = wanted_s[n - k, 1, me]
            a = hd[first].astype(f32)
            b = hd[second].astype(f32)
            if hop > 0:
                row_copy(hop - 1, k).wait_send()
            send[k] = jnp.where(left, a, b).astype(bf16)
            row_copy(hop, k).start()
        row_loop(body)

    def spread(packed):
        p = packed.astype(f32)
        return jnp.concatenate([jnp.where(left, p, 0.0), jnp.where(left, 0.0, p)], axis=0).astype(bf16)

    def head_product(stage):
        return jnp.dot(head_w[stage], heads[stage].reshape(nc * width, nodes), preferred_element_type=f32)

    parts = cells.shape[0]
    cell = srcs[...] * BPD + rows[...]
    for p in range(parts):
        lanes = min(BLK, slots - p * BLK)
        if lanes < BLK:
            cells[p] = jnp.full((1, BLK), -1, jnp.int32)
        cells[p, :, :lanes] = cell[:, p * BLK : p * BLK + lanes]
    down = lax.broadcasted_iota(jnp.int32, (BLK, BLK), 0)
    across = lax.broadcasted_iota(jnp.int32, (BLK, BLK), 1)
    columns = [jnp.broadcast_to(cells[p], (BLK, BLK)).T for p in range(parts)]

    def latest(found):
        best = found[0]
        for f in found[1:]:
            best = jnp.maximum(best, f)
        best = jnp.max(best, axis=0, keepdims=True)
        return jnp.where(best < 0, slots, best)

    for q in range(parts):
        links_v[q] = latest([
            jnp.where((columns[p] == cells[q]) & (down + p * BLK < across + q * BLK), down + p * BLK, -1)
            for p in range(q + 1)])
    live = count[0]
    for q in range(links.shape[0] - parts):
        links_v[parts + q] = latest([
            jnp.where((columns[p] == across + q * BLK) & (down + p * BLK < live), down + p * BLK, -1)
            for p in range(parts)])
    links_copy = pltpu.make_async_copy(links_v, links, table_sem.at[1])
    links_copy.start()

    x = feat[...].astype(f32)
    xs[...] = x
    stat(0, x)

    pl.semaphore_wait(barrier, n - 1 + nc - 1)
    row_loop(lambda k: wanted_copy(k).start())
    for k in range(1, nc):
        square_copy(0, k).start()
    sums[slots] = jnp.zeros((BLK, BLK), f32)
    links_copy.wait()
    vals_copy.wait()

    def link(t, c):
        sums[t] = vals[t].astype(f32) + sums[links[t // BLK, 0, t % BLK]]
        return c

    early = slots * 3 // 8
    lax.fori_loop(0, early, link, 0, unroll=4)
    row_loop(lambda k: wanted_copy(k).wait_recv())
    table = pltpu.make_async_copy(wanted_v.at[pl.ds(1, n - 1)], wanted_s.at[pl.ds(1, n - 1)], table_sem.at[0])
    table.start()
    normalized(0)
    table.wait()
    send_rows(0)
    start_heads(0)

    lax.fori_loop(early, slots, link, 0, unroll=4)

    def lay(q, c):
        for r in range(BPD):
            for h in range(2):
                at = (2 * q + h) * BPD + r
                dense[q, r * BLK : (r + 1) * BLK, h * BLK : (h + 1) * BLK] = (
                    sums[links[parts + at // BLK, 0, at % BLK]].astype(bf16))
        return c

    lax.fori_loop(0, dense.shape[0], lay, 0)

    weight_copy.wait()
    depth = weight_v.shape[1]
    pick = (lax.broadcasted_iota(jnp.int32, (width, depth), 1)
            == lax.broadcasted_iota(jnp.int32, (width, depth), 0) + col * width).astype(f32).astype(bf16)
    for stage in range(HOPS + 1):
        head_w[stage] = lax.dot_general(
            pick, weight_v[stage], (((1,), (1,)), ((), ())), preferred_element_type=f32).astype(bf16)
    noise_copy.wait()

    for hop in range(HOPS):
        acc[...] = jnp.dot(dense[0], spread(hp[0]), preferred_element_type=f32)
        for j in range(1, PAIRS):
            acc[...] += jnp.dot(dense[j], spread(hp[j]), preferred_element_type=f32)
        if hop == 1:
            wait_heads(0)
            enc[...] = head_product(0)
        elif hop > 1:
            wait_heads(hop - 1)
            enc[...] += head_product(hop - 1)

        def arrive(k):
            row_copy(hop, k).wait_recv()
            owner = lax.rem(me + n - k, n)
            acc[...] += jnp.dot(dense[PAIRS + owner], spread(recv[hop, k]), preferred_element_type=f32)

        row_loop(arrive)
        for r in range(BPD):
            g = acc[block(r), :].T
            xs[:, block(r)] = g[:width] + g[width:] + noise_v[hop, :, block(r)]
        x = xs[...]
        stat(hop + 1, x)
        for k in range(1, nc):
            square_copy(hop + 1, k).start()
        if hop + 1 < HOPS:
            normalized(hop + 1)
            send_rows(hop + 1)
        else:
            heads[HOPS, col] = x.astype(bf16)
        start_heads(hop + 1)

    wait_heads(HOPS - 1)
    enc[...] += head_product(HOPS - 1)
    inverse = inverse_norm(HOPS)
    wait_heads(HOPS)
    out[...] = (enc[...] + head_product(HOPS) * inverse).astype(bf16)

    row_loop(lambda k: wanted_copy(k).wait_send())
    row_loop(lambda k: row_copy(HOPS - 1, k).wait_send())
    for stage in range(HOPS + 1):
        for k in range(1, nc):
            square_copy(stage, k).wait_send()
            head_copy(stage, k, col).wait_send()


def shards(n, nc, features, tile_vals, tile_rows, tile_srcs, tile_count, needed, hop_noise, enc_weight):
    local_rows, width = features.shape
    slots = tile_vals.shape[0]
    parts = pl.cdiv(slots, BLK)
    groups = pl.cdiv((BPD + n * CAP) * BPD, BLK)
    f32, bf16 = jnp.float32, jnp.bfloat16
    vmem = pl.BlockSpec(memory_space=pltpu.VMEM)
    smem = pl.BlockSpec(memory_space=pltpu.SMEM)
    anyspace = pl.BlockSpec(memory_space=pl.ANY)
    sem = pltpu.SemaphoreType.DMA
    pair = (BLK, 2 * width)
    result = pl.pallas_call(
        functools.partial(kernel, n, nc),
        out_shape=jax.ShapeDtypeStruct((width, local_rows), bf16),
        in_specs=[vmem, vmem, smem, anyspace, vmem, anyspace, anyspace, anyspace],
        out_specs=vmem,
        scratch_shapes=[
            pltpu.VMEM(tile_vals.shape, bf16),
            pltpu.VMEM((slots + 1, BLK, BLK), f32),
            pltpu.VMEM((PAIRS + n, local_rows, 2 * BLK), bf16),
            pltpu.VMEM((HOPS, width, local_rows), f32),
            pltpu.VMEM(enc_weight.shape, bf16),
            pltpu.VMEM((HOPS + 1, nc, 1, local_rows), f32),
            pltpu.VMEM((width, local_rows), f32),
            pltpu.VMEM((PAIRS,) + pair, bf16),
            pltpu.VMEM((BPD,) + pair, bf16),
            pltpu.VMEM((n,) + pair, bf16),
            pltpu.VMEM((HOPS, n) + pair, bf16),
            pltpu.VMEM((n, CAP, n), jnp.int32),
            pltpu.SMEM((n, CAP, n), jnp.int32),
            pltpu.VMEM((parts, 1, BLK), jnp.int32),
            pltpu.VMEM((parts + groups, 1, BLK), jnp.int32),
            pltpu.SMEM((parts + groups, 1, BLK), jnp.int32),
            pltpu.VMEM((HOPS + 1, nc, width, local_rows), bf16),
            pltpu.VMEM((HOPS + 1, width, nc * width), bf16),
            pltpu.VMEM((local_rows, 2 * width), f32),
            pltpu.VMEM((width, local_rows), f32),
            sem((3,)),
            sem((n,)), sem((n,)),
            sem((HOPS + 1, nc)), sem((HOPS + 1, nc)),
            sem((HOPS, n)), sem((HOPS, n)),
            sem((HOPS + 1, nc)), sem((HOPS + 1, nc)),
            sem((2,)),
        ],
        compiler_params=pltpu.CompilerParams(
            collective_id=0, has_side_effects=True, vmem_limit_bytes=62 * 2**20),
    )(tile_rows, tile_srcs, tile_count, needed.transpose(0, 2, 1), features.T, tile_vals,
      hop_noise.transpose(0, 2, 1), enc_weight)
    return result.T


def solution(mesh):
    n, nc = mesh.shape["row"], mesh.shape["col"]
    in_specs = (
        P("row", "col"),
        P("row", None, None),
        P("row", None),
        P("row", None),
        P("row"),
        P("row", None, None),
        P(None, "row", "col"),
        P(),
    )
    return jax.shard_map(functools.partial(shards, n, nc), mesh=mesh, in_specs=in_specs,
                         out_specs=P("row", "col"), check_vma=False)
```

time: 52 us -> 39.6 us (0.76)
  local copies, waits for them, and re-layouts: 7.21 us -> 1.57 us
  Pallas kernels: 41.7 us -> 37.2 us
  other arithmetic: 2.18 us -> 0 us
    pallas_call x1, Pallas kernels: 41.7 us -> 37.2 us  [shards(): pl.pallas_call(functools.partial(kernel, n, nc), out_shape=jax.ShapeDtype...]
    unnamed x2 -> x1, local copies, waits for them, and re-layouts: 4.13 us -> 1.57 us
    pallas_call x1 -> x0, local copies, waits for them, and re-layouts: 1.73 us -> none  [shards(): pl.pallas_call(functools.partial(kernel, n, nc), out_shape=jax.ShapeDtype...]
    select_n x2 -> x0, other arithmetic: 1.16 us -> none  [the longest x1 0.58 us: shards(): head = jnp.where(head < 0, slots, head)]
    another operation x1 -> x0, local copies, waits for them, and re-layouts: 0.75 us -> none  [shards(): wanted = jnp.pad(needed[0][:, None, :], ((0, 0), (0, 0), (0, BLK - CAP)))]
    add x1 -> x0, other arithmetic: 0.7 us -> none  [shards(): cell = tile_srcs[0] * BPD + tile_rows[0]]
    pad x1 -> x0, local copies, waits for them, and re-layouts: 0.6 us -> none  [shards(): wanted = jnp.pad(needed[0][:, None, :], ((0, 0), (0, 0), (0, BLK - CAP)))]
where the time goes in v2:
time: 39.6 us; the launch traced here: 39.4 us
  Pallas kernels  37.2 us (94%)
  local copies, waits for them, and re-layouts  1.57 us (4%)
  between operations  0.66 us (2%)
    pallas_call x1, Pallas kernels, shards(): pl.pallas_call(functools.partial(kernel, n, nc), out_shape=jax.ShapeDtype...  37.2 us
    unnamed x1, local copies, waits for them, and re-layouts  1.57 us

profile of v2, /device:TPU:1, one launch (start us, length us, event | category | flops | bytes accessed | tf_op | source)
XLA Modules:
  0.0 39.4 jit_solution(12135214202868100766)
XLA Ops:
  0.7 37.2 %shard_map.82 = bf16[64,1024]{1,0:T(8,128)(2,1)} custom-call(s32[1,160]{1,0:T(1,128)} %rows.1, s32[1,160]{1,0:T(1,128)} %srcs.1, s32[1]{0:T(128)S(6)} %copy.10.count, s32[1,2,8]{2,1,0:T(2,128)} %bitcast.7, bf16[64,1024]{1,0:T(8,128)(2,1)} %bitcast.6, bf16[160,128,128]{2,1,0:T(8,128)(2,1)} %tiles.1, f32[2,64,1024]{2,1,0:T(8,128)} %bitcast.4, ...), custom_call_target="tpu_custom_call" | custom-call | tf_op jit(solution)/shard_map/pallas_call | solution.py:263
  37.8 1.6 %copy.11 = bf16[1024,64]{0,1:T(8,128)(2,1)} copy(bf16[1024,64]{0,1:T(8,128)(2,1)} %bitcast.5) | data formatting | bytes 262144

commit v3 on v2

--- a/solution.py
+++ b/solution.py
@@ -17,12 +17,14 @@
 
 
 def kernel(n, nc, rows, srcs, count, wanted, feat, tiles, noise, weight, out,
-           vals, sums, dense, noise_v, weight_v, squares, xs, hp, hd, send, recv, wanted_v, wanted_s,
-           cells, links_v, links, heads, head_w, acc, enc,
-           local_sem, wanted_send, wanted_recv, sq_send, sq_recv, row_send, row_recv, col_send, col_recv, table_sem):
+           vals, sums, dense, noise_v, weight_v, squares, xs, hp, raw, scale, send, recv, scale_send, scale_recv, wanted_v, wanted_s,
+           cells, links_v, links, heads, last, head_w, acc, enc,
+           local_sem, wanted_send, wanted_recv, sq_send, sq_recv, row_send, row_recv, tail_send, tail_recv,
+           col_send, col_recv, last_send, last_recv, table_sem):
     me = lax.axis_index("row")
     col = lax.axis_index("col")
     width, nodes = feat.shape
+    half = nodes // 2
     slots = vals.shape[0]
     f32, bf16 = jnp.float32, jnp.bfloat16
 
@@ -86,6 +88,21 @@
             send_sem=row_send.at[hop, k], recv_sem=row_recv.at[hop, k],
             device_id={"row": lax.rem(me + k, n)}, device_id_type=MESH)
 
+    def scale_copy(hop, k):
+        return pltpu.make_async_remote_copy(
+            src_ref=scale_send.at[hop, k], dst_ref=scale_recv.at[hop, k],
+            send_sem=tail_send.at[hop, k], recv_sem=tail_recv.at[hop, k],
+            device_id={"row": lax.rem(me + k, n)}, device_id_type=MESH)
+
+    def last_copy(part, way, source, peer):
+        return pltpu.make_async_remote_copy(
+            src_ref=last.at[part, source], dst_ref=last.at[part, source],
+            send_sem=last_send.at[part, way], recv_sem=last_recv.at[part, way],
+            device_id={"col": peer}, device_id_type=MESH)
+
+    def far_first(i):
+        return n // 2 + (1 - 2 * lax.rem(i, 2)) * ((i + 1) // 2)
+
     def inverse_norm(stage):
         for k in range(1, nc):
             square_copy(stage, k).wait_recv()
@@ -96,29 +113,35 @@
 
     def normalized(stage):
         inverse = inverse_norm(stage)
+        for r in range(BPD):
+            scale[r] = inverse[:, block(r)]
         for j in range(PAIRS):
             a, b = block(2 * j), block(2 * j + 1)
             ha = (xs[:, a] * inverse[:, a]).astype(bf16)
             hb = (xs[:, b] * inverse[:, b]).astype(bf16)
             heads[stage, col, :, a] = ha
             heads[stage, col, :, b] = hb
-            h = jnp.concatenate([ha.astype(f32), hb.astype(f32)], axis=0).T
-            hp[j] = h.astype(bf16)
-            turned = pltpu.roll(h, width, 1)
-            hd[2 * j] = jnp.where(left, h, turned).astype(bf16)
-            hd[2 * j + 1] = jnp.where(left, turned, h).astype(bf16)
+            hp[j] = jnp.concatenate([ha.astype(f32), hb.astype(f32)], axis=0).T.astype(bf16)
 
     def send_rows(hop):
-        def body(k):
-            first = wanted_s[n - k, 0, me]
-            second = wanted_s[n - k, 1, me]
-            a = hd[first].astype(f32)
-            b = hd[second].astype(f32)
+        def body(i, c):
+            k = far_first(i)
             if hop > 0:
                 row_copy(hop - 1, k).wait_send()
-            send[k] = jnp.where(left, a, b).astype(bf16)
+            send[k, :width] = raw[wanted_s[n - k, 0, me]]
+            send[k, width:] = raw[wanted_s[n - k, 1, me]]
             row_copy(hop, k).start()
-        row_loop(body)
+            return c
+        lax.fori_loop(0, n - 1, body, 0)
+
+    def send_scales(hop):
+        def body(i, c):
+            k = far_first(i)
+            scale_send[hop, k, 0] = scale[wanted_s[n - k, 0, me]]
+            scale_send[hop, k, 1] = scale[wanted_s[n - k, 1, me]]
+            scale_copy(hop, k).start()
+            return c
+        lax.fori_loop(0, n - 1, body, 0)
 
     def spread(packed):
         p = packed.astype(f32)
@@ -159,6 +182,8 @@
 
     x = feat[...].astype(f32)
     xs[...] = x
+    for r in range(BPD):
+        raw[r] = feat[:, block(r)]
     stat(0, x)
 
     pl.semaphore_wait(barrier, n - 1 + nc - 1)
@@ -178,9 +203,10 @@
     row_loop(lambda k: wanted_copy(k).wait_recv())
     table = pltpu.make_async_copy(wanted_v.at[pl.ds(1, n - 1)], wanted_s.at[pl.ds(1, n - 1)], table_sem.at[0])
     table.start()
-    normalized(0)
     table.wait()
     send_rows(0)
+    normalized(0)
+    send_scales(0)
     start_heads(0)
 
     lax.fori_loop(early, slots, link, 0, unroll=4)
@@ -215,38 +241,70 @@
             wait_heads(hop - 1)
             enc[...] += head_product(hop - 1)
 
-        def arrive(k):
+        def arrive(i, c):
+            k = far_first(n - 2 - i)
             row_copy(hop, k).wait_recv()
+            scale_copy(hop, k).wait_recv()
+            both = jnp.concatenate(
+                [jnp.broadcast_to(scale_recv[hop, k, 0], (width, BLK)),
+                 jnp.broadcast_to(scale_recv[hop, k, 1], (width, BLK))], axis=0)
+            h = (recv[hop, k].astype(f32) * both).astype(bf16)
             owner = lax.rem(me + n - k, n)
-            acc[...] += jnp.dot(dense[PAIRS + owner], spread(recv[hop, k]), preferred_element_type=f32)
-
-        row_loop(arrive)
+            acc[...] += jnp.dot(dense[PAIRS + owner], spread(h.astype(f32).T), preferred_element_type=f32)
+            return c
+
+        lax.fori_loop(0, n - 1, arrive, 0)
         for r in range(BPD):
             g = acc[block(r), :].T
-            xs[:, block(r)] = g[:width] + g[width:] + noise_v[hop, :, block(r)]
-        x = xs[...]
-        stat(hop + 1, x)
+            x = g[:width] + g[width:] + noise_v[hop, :, block(r)]
+            xs[:, block(r)] = x
+            if hop + 1 < HOPS:
+                raw[r] = x.astype(bf16)
+            else:
+                last[r * BLK // half, col, :, r * BLK % half : r * BLK % half + BLK] = x.astype(bf16)
+        if hop + 1 < HOPS:
+            send_rows(hop + 1)
+        stat(hop + 1, xs[...])
         for k in range(1, nc):
             square_copy(hop + 1, k).start()
         if hop + 1 < HOPS:
             normalized(hop + 1)
-            send_rows(hop + 1)
-        else:
-            heads[HOPS, col] = x.astype(bf16)
-        start_heads(hop + 1)
-
+            send_scales(hop + 1)
+            start_heads(hop + 1)
+
+    near = col + 1 - 2 * lax.rem(col, 2)
+    far = lax.rem(col + 2, nc)
+    both = lax.rem(near + 2, nc)
+    for part in range(2):
+        last_copy(part, 0, col, far).start()
+    for part in range(2):
+        last_copy(part, 1, col, near).start()
     wait_heads(HOPS - 1)
     enc[...] += head_product(HOPS - 1)
     inverse = inverse_norm(HOPS)
-    wait_heads(HOPS)
-    out[...] = (enc[...] + head_product(HOPS) * inverse).astype(bf16)
+    for part in range(2):
+        last_copy(part, 0, far, far).wait_recv()
+        last_copy(part, 2, far, near).start()
+    for part in range(2):
+        lanes = slice(part * half, (part + 1) * half)
+        last_copy(part, 1, near, near).wait_recv()
+        last_copy(part, 2, both, near).wait_recv()
+        product = jnp.dot(head_w[HOPS], last[part].reshape(nc * width, half), preferred_element_type=f32)
+        out[:, lanes] = enc[:, lanes] + product * inverse[:, lanes]
 
     row_loop(lambda k: wanted_copy(k).wait_send())
     row_loop(lambda k: row_copy(HOPS - 1, k).wait_send())
     for stage in range(HOPS + 1):
         for k in range(1, nc):
             square_copy(stage, k).wait_send()
+    for stage in range(HOPS):
+        row_loop(lambda k: scale_copy(stage, k).wait_send())
+        for k in range(1, nc):
             head_copy(stage, k, col).wait_send()
+    for part in range(2):
+        last_copy(part, 0, col, far).wait_send()
+        last_copy(part, 1, col, near).wait_send()
+        last_copy(part, 2, far, near).wait_send()
 
 
 def shards(n, nc, features, tile_vals, tile_rows, tile_srcs, tile_count, needed, hop_noise, enc_weight):
@@ -262,7 +320,7 @@
     pair = (BLK, 2 * width)
     result = pl.pallas_call(
         functools.partial(kernel, n, nc),
-        out_shape=jax.ShapeDtypeStruct((width, local_rows), bf16),
+        out_shape=jax.ShapeDtypeStruct((width, local_rows), f32),
         in_specs=[vmem, vmem, smem, anyspace, vmem, anyspace, anyspace, anyspace],
         out_specs=vmem,
         scratch_shapes=[
@@ -274,15 +332,19 @@
             pltpu.VMEM((HOPS + 1, nc, 1, local_rows), f32),
             pltpu.VMEM((width, local_rows), f32),
             pltpu.VMEM((PAIRS,) + pair, bf16),
-            pltpu.VMEM((BPD,) + pair, bf16),
-            pltpu.VMEM((n,) + pair, bf16),
-            pltpu.VMEM((HOPS, n) + pair, bf16),
+            pltpu.VMEM((BPD, width, BLK), bf16),
+            pltpu.VMEM((BPD, 1, BLK), f32),
+            pltpu.VMEM((n, 2 * width, BLK), bf16),
+            pltpu.VMEM((HOPS, n, 2 * width, BLK), bf16),
+            pltpu.VMEM((HOPS, n, CAP, 1, BLK), f32),
+            pltpu.VMEM((HOPS, n, CAP, 1, BLK), f32),
             pltpu.VMEM((n, CAP, n), jnp.int32),
             pltpu.SMEM((n, CAP, n), jnp.int32),
             pltpu.VMEM((parts, 1, BLK), jnp.int32),
             pltpu.VMEM((parts + groups, 1, BLK), jnp.int32),
             pltpu.SMEM((parts + groups, 1, BLK), jnp.int32),
-            pltpu.VMEM((HOPS + 1, nc, width, local_rows), bf16),
+            pltpu.VMEM((HOPS, nc, width, local_rows), bf16),
+            pltpu.VMEM((2, nc, width, local_rows // 2), bf16),
             pltpu.VMEM((HOPS + 1, width, nc * width), bf16),
             pltpu.VMEM((local_rows, 2 * width), f32),
             pltpu.VMEM((width, local_rows), f32),
@@ -290,14 +352,16 @@
             sem((n,)), sem((n,)),
             sem((HOPS + 1, nc)), sem((HOPS + 1, nc)),
             sem((HOPS, n)), sem((HOPS, n)),
-            sem((HOPS + 1, nc)), sem((HOPS + 1, nc)),
+            sem((HOPS, n)), sem((HOPS, n)),
+            sem((HOPS, nc)), sem((HOPS, nc)),
+            sem((2, 3)), sem((2, 3)),
             sem((2,)),
         ],
         compiler_params=pltpu.CompilerParams(
             collective_id=0, has_side_effects=True, vmem_limit_bytes=62 * 2**20),
     )(tile_rows, tile_srcs, tile_count, needed.transpose(0, 2, 1), features.T, tile_vals,
       hop_noise.transpose(0, 2, 1), enc_weight)
-    return result.T
+    return result.T.astype(bf16)
 
 
 def solution(mesh):

time: 39.6 us -> 40 us (1.010)
  other arithmetic: 0 us -> 1.62 us
  local copies, waits for them, and re-layouts: 1.57 us -> 0 us
    convert_element_type x0 -> x1, other arithmetic: none -> 1.62 us  [shards(): return result.T.astype(bf16)]
    unnamed x1 -> x0, local copies, waits for them, and re-layouts: 1.57 us -> none
where the time goes in v3:
time: 40 us; the launch traced here: 39.8 us
  Pallas kernels  37.5 us (94%)
  other arithmetic  1.62 us (4%)
  between operations  0.66 us (2%)
    pallas_call x1, Pallas kernels, shards(): pl.pallas_call(functools.partial(kernel, n, nc), out_shape=jax.ShapeDtype...  37.5 us
    convert_element_type x1, other arithmetic, shards(): return result.T.astype(bf16)  1.62 us

profile of v3, /device:TPU:1, one launch (start us, length us, event | category | flops | bytes accessed | tf_op | source)
XLA Modules:
  0.0 39.8 jit_solution(6787856448393344572)
XLA Ops:
  0.7 37.5 %shard_map.82 = f32[64,1024]{1,0:T(8,128)} custom-call(s32[1,160]{1,0:T(1,128)} %rows.1, s32[1,160]{1,0:T(1,128)} %srcs.1, s32[1]{0:T(128)S(6)} %copy.9.count, s32[1,2,8]{2,1,0:T(2,128)} %bitcast.7, bf16[64,1024]{1,0:T(8,128)(2,1)} %bitcast.6, bf16[160,128,128]{2,1,0:T(8,128)(2,1)} %tiles.1, f32[2,64,1024]{2,1,0:T(8,128)} %bitcast.5, bf16[3,256,256]{2,1,0:T(8,128)(2,1)} %weight.1), custom_call_target="tpu_custom_call" | custom-call | tf_op jit(solution)/shard_map/pallas_call | solution.py:321
  38.2 1.6 %convert_bitcast_fusion = bf16[1024,64]{0,1:T(8,128)(2,1)} fusion(f32[64,1024]{1,0:T(8,128)} %shard_map.82), kind=kLoop, calls=%fused_computation | loop fusion | flops 65536 | bytes 393216 | tf_op jit(solution)/shard_map/convert_element_type | solution.py:364

commit v4 on v3

--- a/solution.py
+++ b/solution.py
@@ -17,7 +17,7 @@
 
 
 def kernel(n, nc, rows, srcs, count, wanted, feat, tiles, noise, weight, out,
-           vals, sums, dense, noise_v, weight_v, squares, xs, hp, raw, scale, send, recv, scale_send, scale_recv, wanted_v, wanted_s,
+           vals, sums, dense, noise_v, weight_v, squares, xs, raw, scale, send, recv, scale_send, scale_recv, wanted_v, wanted_s,
            cells, links_v, links, heads, last, head_w, acc, enc,
            local_sem, wanted_send, wanted_recv, sq_send, sq_recv, row_send, row_recv, tail_send, tail_recv,
            col_send, col_recv, last_send, last_recv, table_sem):
@@ -48,8 +48,6 @@
     noise_copy.start()
     weight_copy.start()
 
-    left = lax.broadcasted_iota(jnp.int32, (BLK, 2 * width), 1) < width
-
     def block(b):
         return slice(b * BLK, (b + 1) * BLK)
 
@@ -115,13 +113,7 @@
         inverse = inverse_norm(stage)
         for r in range(BPD):
             scale[r] = inverse[:, block(r)]
-        for j in range(PAIRS):
-            a, b = block(2 * j), block(2 * j + 1)
-            ha = (xs[:, a] * inverse[:, a]).astype(bf16)
-            hb = (xs[:, b] * inverse[:, b]).astype(bf16)
-            heads[stage, col, :, a] = ha
-            heads[stage, col, :, b] = hb
-            hp[j] = jnp.concatenate([ha.astype(f32), hb.astype(f32)], axis=0).T.astype(bf16)
+        heads[stage, col] = (xs[...] * inverse).astype(bf16)
 
     def send_rows(hop):
         def body(i, c):
@@ -143,9 +135,8 @@
             return c
         lax.fori_loop(0, n - 1, body, 0)
 
-    def spread(packed):
-        p = packed.astype(f32)
-        return jnp.concatenate([jnp.where(left, p, 0.0), jnp.where(left, 0.0, p)], axis=0).astype(bf16)
+    def tile_product(rows_t, q):
+        return lax.dot_general(rows_t, dense[q], (((1,), (1,)), ((), ())), preferred_element_type=f32)
 
     def head_product(stage):
         return jnp.dot(head_w[stage], heads[stage].reshape(nc * width, nodes), preferred_element_type=f32)
@@ -231,9 +222,9 @@
     noise_copy.wait()
 
     for hop in range(HOPS):
-        acc[...] = jnp.dot(dense[0], spread(hp[0]), preferred_element_type=f32)
-        for j in range(1, PAIRS):
-            acc[...] += jnp.dot(dense[j], spread(hp[j]), preferred_element_type=f32)
+        acc[...] = noise_v[hop]
+        for j in range(PAIRS):
+            acc[...] += tile_product(heads[hop, col, :, 2 * j * BLK : (2 * j + 2) * BLK], j)
         if hop == 1:
             wait_heads(0)
             enc[...] = head_product(0)
@@ -245,18 +236,15 @@
             k = far_first(n - 2 - i)
             row_copy(hop, k).wait_recv()
             scale_copy(hop, k).wait_recv()
-            both = jnp.concatenate(
-                [jnp.broadcast_to(scale_recv[hop, k, 0], (width, BLK)),
-                 jnp.broadcast_to(scale_recv[hop, k, 1], (width, BLK))], axis=0)
-            h = (recv[hop, k].astype(f32) * both).astype(bf16)
+            first = (recv[hop, k, :width].astype(f32) * scale_recv[hop, k, 0]).astype(bf16)
+            second = (recv[hop, k, width:].astype(f32) * scale_recv[hop, k, 1]).astype(bf16)
             owner = lax.rem(me + n - k, n)
-            acc[...] += jnp.dot(dense[PAIRS + owner], spread(h.astype(f32).T), preferred_element_type=f32)
+            acc[...] += tile_product(jnp.concatenate([first, second], axis=1), PAIRS + owner)
             return c
 
         lax.fori_loop(0, n - 1, arrive, 0)
         for r in range(BPD):
-            g = acc[block(r), :].T
-            x = g[:width] + g[width:] + noise_v[hop, :, block(r)]
+            x = acc[:, block(r)]
             xs[:, block(r)] = x
             if hop + 1 < HOPS:
                 raw[r] = x.astype(bf16)
@@ -317,7 +305,6 @@
     smem = pl.BlockSpec(memory_space=pltpu.SMEM)
     anyspace = pl.BlockSpec(memory_space=pl.ANY)
     sem = pltpu.SemaphoreType.DMA
-    pair = (BLK, 2 * width)
     result = pl.pallas_call(
         functools.partial(kernel, n, nc),
         out_shape=jax.ShapeDtypeStruct((width, local_rows), f32),
@@ -331,7 +318,6 @@
             pltpu.VMEM(enc_weight.shape, bf16),
             pltpu.VMEM((HOPS + 1, nc, 1, local_rows), f32),
             pltpu.VMEM((width, local_rows), f32),
-            pltpu.VMEM((PAIRS,) + pair, bf16),
             pltpu.VMEM((BPD, width, BLK), bf16),
             pltpu.VMEM((BPD, 1, BLK), f32),
             pltpu.VMEM((n, 2 * width, BLK), bf16),
@@ -346,7 +332,7 @@
             pltpu.VMEM((HOPS, nc, width, local_rows), bf16),
             pltpu.VMEM((2, nc, width, local_rows // 2), bf16),
             pltpu.VMEM((HOPS + 1, width, nc * width), bf16),
-            pltpu.VMEM((local_rows, 2 * width), f32),
+            pltpu.VMEM((width, local_rows), f32),
             pltpu.VMEM((width, local_rows), f32),
             sem((3,)),
             sem((n,)), sem((n,)),

time: 40 us -> 39.1 us (0.978)
  Pallas kernels: 37.5 us -> 36.7 us
    pallas_call x1, Pallas kernels: 37.5 us -> 36.7 us  [shards(): pl.pallas_call(functools.partial(kernel, n, nc), out_shape=jax.ShapeDtype...]
where the time goes in v4:
time: 39.1 us; the launch traced here: 38.9 us
  Pallas kernels  36.7 us (94%)
  other arithmetic  1.62 us (4%)
  between operations  0.66 us (2%)
    pallas_call x1, Pallas kernels, shards(): pl.pallas_call(functools.partial(kernel, n, nc), out_shape=jax.ShapeDtype...  36.7 us
    convert_element_type x1, other arithmetic, shards(): return result.T.astype(bf16)  1.62 us

profile of v4, /device:TPU:1, one launch (start us, length us, event | category | flops | bytes accessed | tf_op | source)
XLA Modules:
  0.0 38.9 jit_solution(9424087303342219967)
XLA Ops:
  0.7 36.7 %shard_map.82 = f32[64,1024]{1,0:T(8,128)} custom-call(s32[1,160]{1,0:T(1,128)} %rows.1, s32[1,160]{1,0:T(1,128)} %srcs.1, s32[1]{0:T(128)S(6)} %copy.9.count, s32[1,2,8]{2,1,0:T(2,128)} %bitcast.7, bf16[64,1024]{1,0:T(8,128)(2,1)} %bitcast.6, bf16[160,128,128]{2,1,0:T(8,128)(2,1)} %tiles.1, f32[2,64,1024]{2,1,0:T(8,128)} %bitcast.5, bf16[3,256,256]{2,1,0:T(8,128)(2,1)} %weight.1), custom_call_target="tpu_custom_call" | custom-call | tf_op jit(solution)/shard_map/pallas_call | solution.py:308
  37.3 1.6 %convert_bitcast_fusion = bf16[1024,64]{0,1:T(8,128)(2,1)} fusion(f32[64,1024]{1,0:T(8,128)} %shard_map.82), kind=kLoop, calls=%fused_computation | loop fusion | flops 65536 | bytes 393216 | tf_op jit(solution)/shard_map/convert_element_type | solution.py:350
